TPU v7x, 32 devices: a whole 2x2x4 slice. The times are simulated.
32 devices in a mesh: dp: 8 (over z, y), tensor: 4 (over x, core).
Axes of the slice: x: 2, y: 2, z: 4, core: 2. Of those that a mesh axis runs over, the one named last changes fastest.
Arguments:
- acts: bfloat16 [4096, 4096], P('dp'), may hold values from -0.25 to 0.25
- up_cot: bfloat16 [4096, 3584], P('dp', 'tensor'), may hold values from -6 to 6
- up_weight: bfloat16 [4096, 3584], P(None, 'tensor'), may hold values from -0.09375 to 0.09375
- error_buf: bfloat16 [8, 4096, 3584], P('dp', None, 'tensor'), may hold values from -4 to 4
- q_init: float32 [64, 3584], P(None, 'tensor'), may hold values from -6 to 6
Outputs:
- input_grad: bfloat16 [4096, 4096], P(('dp', 'tensor'))
- new_error: bfloat16 [8, 4096, 3584], P('dp', None, 'tensor')
- p_factor: float32 [64, 4096], replicated
- q_factor: float32 [64, 3584], P(None, 'tensor')
All inputs are finite; a program needn't handle non-finite values.
Results may differ from a plain program's by a relative error of at most 0.001.
Values sent between devices are 32-bit elements; how exact they have to be, the bound alone decides.
A program may use at most 128 MiB of HBM per device.

v0:
```python
import jax
import jax.numpy as jnp
from jax import lax
from jax.sharding import PartitionSpec as P


def body(acts, up_cot, up_weight, error_buf, q_init):
    highest = lax.Precision.HIGHEST
    n_replicas = lax.axis_size("dp")
    input_grad = lax.psum_scatter(
        lax.dot_general(
            up_cot, up_weight, (((1,), (1,)), ((), ())), preferred_element_type=jnp.float32
        ),
        "tensor",
        scatter_dimension=0,
        tiled=True,
    ).astype(jnp.bfloat16)
    grad = lax.dot_general(
        acts, up_cot, (((0,), (0,)), ((), ())), preferred_element_type=jnp.float32
    )
    merged = grad + error_buf[0].astype(jnp.float32)
    left_term = lax.dot_general(q_init, merged, (((1,), (1,)), ((), ())), precision=highest)
    left = lax.psum(left_term, ("dp", "tensor"))
    gram = jnp.dot(left, left.T, precision=highest)
    chol = jnp.linalg.cholesky(gram)
    basis = lax.linalg.triangular_solve(chol, left, left_side=True, lower=True)
    right_term = jnp.dot(basis, merged, precision=highest)
    q_factor = lax.psum(right_term, "dp") / n_replicas
    approx = lax.dot_general(basis, q_factor, (((0,), (0,)), ((), ())), precision=highest)
    new_error = (merged - approx).astype(jnp.bfloat16)[None]
    return (input_grad, new_error, basis, q_factor)


def solution(mesh):
    return jax.shard_map(
        body,
        mesh=mesh,
        in_specs=(
            P("dp", None),
            P("dp", "tensor"),
            P(None, "tensor"),
            P("dp", None, "tensor"),
            P(None, "tensor"),
        ),
        out_specs=(P(("dp", "tensor"), None), P("dp", None, "tensor"), P(), P(None, "tensor")),
        check_vma=False,
    )
```

profile of v0, /device:TPU:0, one launch (start us, length us, event | category | flops | bytes accessed | tf_op | source)
XLA Modules:
  0.0 299.3 jit_solution(8984752796776675170)
XLA Ops:
  8.0 0.0 all-reduce.3.cloned.1.call-start
  8.1 1.1 copy-done
  9.2 10.4 %convert_add_fusion = f32[4096,896]{1,0:T(8,128)S(1)} fusion(bf16[1,4096,896]{2,1,0:T(8,128)(2,1)} %param.8, bf16[512,4096]{1,0:T(8,128)(2,1)} %param.5, bf16[512,896]{1,0:T(8,128)(2,1)S(1)} %copy-done), kind=kOutput, calls=%fused_computation | convolution fusion | flops 3765436416 | bytes 27131904 | tf_op jit(solution)/shard_map/dot_general | solution.py:18
  19.6 5.2 %copy-done.1 = f32[4096,896]{1,0:T(8,128)} copy-done((f32[4096,896]{1,0:T(8,128)}, f32[4096,896]{1,0:T(8,128)S(1)}, u32[]{:S(2)}) %copy-start.1) | copy-done | bytes 14680088
  24.8 15.5 %convolution_bitcast_fusion = f32[64,4096]{1,0:T(8,128)} fusion(f32[4096,896]{1,0:T(8,128)S(1)} %convert_add_fusion, f32[64,896]{1,0:T(8,128)S(1)} %copy-done.4), kind=kOutput, calls=%fused_computation.3 | convolution fusion | flops 2818572288 | bytes 15958016 | tf_op jit(solution)/shard_map/dot_general | solution.py:22
  40.3 0.0 all-reduce.3.cloned.1.call-update
  40.3 0.3 all-reduce.5.cloned.1.call-start
  40.6 132.4 %all-reduce.3.cloned.1.call-done = f32[64,4096]{1,0:T(8,128)} async-done(((f32[64,4096]{1,0:T(8,128)}), f32[64,4096]{1,0:T(8,128)}) %all-reduce.3.cloned.1.call-update) | async-done | bytes 1048592 | tf_op jit(solution)/shard_map/psum | solution.py:23
  172.9 2.5 fusion.6
  175.5 0.1 copy.9
  175.5 5.8 %cholesky.16 = f32[64,64]{1,0:T(8,128)S(1)} custom-call(f32[64,64]{1,0:T(8,128)S(1)} %fusion.4), custom_call_target="Cholesky" | custom-call | tf_op jit(solution)/shard_map/jit(cholesky)/cholesky | solution.py:25
  181.4 0.6 compare_reduce_fusion
  182.1 0.7 fusion.1
  182.7 4.9 %custom-call.6 = f32[1,64,64]{1,2,0:T(8,128)S(1)} custom-call(f32[1,64,64]{2,1,0:T(8,128)S(1)} %fusion.1), custom_call_target="InvertDiagBlocksLowerTriangular" | custom-call | tf_op jit(solution)/shard_map/triangular_solve | solution.py:26
  187.6 2.3 fusion.2
  189.9 12.7 %fusion.7 = f32[64,896]{1,0:T(8,128)} fusion(f32[64,4096]{1,0:T(8,128)S(1)} %fusion.2, f32[4096,896]{1,0:T(8,128)} %copy-done.1), kind=kOutput, calls=%fused_computation.17 | convolution fusion | flops 2818572288 | bytes 15958016 | tf_op jit(solution)/shard_map/dot_general | solution.py:27
  202.6 0.0 all-reduce.5.cloned.1.call-update
  202.7 0.3 reduce-scatter.2.cloned.1.call-start
  203.0 9.9 %fusion.5 = f32[512,4096]{1,0:T(8,128)} fusion(bf16[512,896]{1,0:T(8,128)(2,1)S(1)} %copy-done, bf16[4096,896]{1,0:T(8,128)(2,1)} %param.7), kind=kOutput, calls=%fused_computation.15 | convolution fusion | flops 3758096384 | bytes 16646144 | tf_op jit(solution)/shard_map/dot_general | solution.py:11
  212.8 0.0 reduce-scatter.2.cloned.1.call-update
  212.9 59.5 %all-reduce.5.cloned.1.call-done = f32[64,896]{1,0:T(8,128)} async-done(((f32[64,896]{1,0:T(8,128)}), f32[64,896]{1,0:T(8,128)}) %all-reduce.5.cloned.1.call-update) | async-done | bytes 229392 | tf_op jit(solution)/shard_map/psum | solution.py:28
  272.3 1.0 broadcast_multiply_fusion
  273.3 15.8 %fusion = bf16[1,4096,896]{2,1,0:T(8,128)(2,1)} fusion(f32[4096,896]{1,0:T(8,128)} %copy-done.1, f32[64,4096]{1,0:T(8,128)S(1)} %fusion.2, f32[64,896]{1,0:T(8,128)S(1)} %broadcast_multiply_fusion), kind=kOutput, calls=%fused_computation.2 | convolution fusion | flops 2825912320 | bytes 23298048 | tf_op jit(solution)/shard_map/dot_general | solution.py:29
  289.1 2.7 convert_element_type.12
  (11 shorter events, 0.1 us)
Async XLA Ops:
  8.0 1.2 copy-start
  8.0 16.8 %copy-start.4 = (f32[64,896]{1,0:T(8,128)S(1)}, f32[64,896]{1,0:T(8,128)}, u32[]{:S(2)}) copy-start(f32[64,896]{1,0:T(8,128)} %param.9) | copy-start | bytes 688132
  8.0 164.9 %all-reduce.3.cloned.1.call-start = ((), (), s32[]{:S(2)}) async-start(), calls=%async_computation.2 | async-start | bytes 2097152 | tf_op jit(solution)/shard_map/psum | solution.py:23
  19.6 5.2 %copy-start.1 = (f32[4096,896]{1,0:T(8,128)}, f32[4096,896]{1,0:T(8,128)S(1)}, u32[]{:S(2)}) copy-start(f32[4096,896]{1,0:T(8,128)S(1)} %convert_add_fusion) | copy-start | bytes 44040196
  40.3 232.0 %all-reduce.5.cloned.1.call-start = ((), (), s32[]{:S(2)}) async-start(), calls=%async_computation.3 | async-start | bytes 458752 | tf_op jit(solution)/shard_map/psum | solution.py:28
  189.9 83.4 %copy-start.2 = (f32[64,4096]{1,0:T(8,128)}, f32[64,4096]{1,0:T(8,128)S(1)}, u32[]{:S(2)}) copy-start(f32[64,4096]{1,0:T(8,128)S(1)} %fusion.2) | copy-start | bytes 3145732
  202.7 86.5 %reduce-scatter.2.cloned.1.call-start = ((), (), s32[]{:S(2)}) async-start(), calls=%async_computation.1 | async-start | bytes 10485760 | tf_op jit(solution)/shard_map/reduce_scatter | solution.py:10
  273.3 15.8 %copy-start.3 = (f32[64,896]{1,0:T(8,128)}, f32[64,896]{1,0:T(8,128)S(1)}, u32[]{:S(2)}) copy-start(f32[64,896]{1,0:T(8,128)S(1)} %broadcast_multiply_fusion) | copy-start | bytes 688132
Sparse Core Ops, SparseCore 0:
  40.4 132.4 all-reduce.2
  202.8 69.4 all-reduce.4
Sparse Core Ops, SparseCore 1:
  212.9 70.6 reduce-scatter.1
where the time goes:
time: 300 us; the launch traced here: 299 us
  waiting for transfers between devices  192 us (64%)
  matrix products  69 us (23%)
  other arithmetic  15.7 us (5%)
  between operations  15.6 us (5%)
  local copies, waits for them, and re-layouts  6.42 us (2%)
    psum x1, waiting for transfers between devices, body(): left = lax.psum(left_term, ('dp', 'tensor'))  132 us
    psum x1, waiting for transfers between devices, body(): q_factor = lax.psum(right_term, 'dp') / n_replicas  59.5 us
    dot_general x1, matrix products, body(): lax.dot_general(basis, q_factor, (((0,), (0,)), ((), ())), precision=high...  15.8 us
    dot_general x1, matrix products, body(): lax.dot_general(q_init, merged, (((1,), (1,)), ((), ())), precision=highest)  15.5 us
    dot_general x1, matrix products, body(): right_term = jnp.dot(basis, merged, precision=highest)  12.7 us
    dot_general x1, matrix products, body(): lax.dot_general(acts, up_cot, (((0,), (0,)), ((), ())), preferred_element...  10.4 us
    dot_general x1, matrix products, body(): lax.dot_general(up_cot, up_weight, (((1,), (1,)), ((), ())), preferred_el...  9.87 us
    another operation x3, other arithmetic, body(): chol = jnp.linalg.cholesky(gram)  6.52 us
  transfers between devices with their start and end apart: 3, of which 2 were waited for; matrix products, arithmetic and copies ran while one was open for 9% of the time, Pallas kernels for 0%

commit v1 on v0

v1 whole, which is shorter than its diff:
```python
import functools

import jax
import jax.numpy as jnp
from jax import lax
from jax.experimental import pallas as pl
from jax.experimental.pallas import tpu as pltpu
from jax.sharding import PartitionSpec as P

F32 = jnp.float32
BF16 = jnp.bfloat16
HI = lax.Precision.HIGHEST
VMEM = pltpu.VMEM
PARAMS = pltpu.CompilerParams(vmem_limit_bytes=56 * 1024 * 1024)
NT = (((1,), (1,)), ((), ()))
NN = (((1,), (0,)), ((), ()))
TN = (((0,), (0,)), ((), ()))


def dot(a, b, dims, precision=None):
    return lax.dot_general(a, b, dims, precision=precision, preferred_element_type=F32)


def halves(x):
    high = x.astype(BF16)
    low = (x - high.astype(F32)).astype(BF16)
    return high, low


def dot_split(x, b, dims):
    rows = x.shape[0]
    both = dot(jnp.concatenate(halves(x), axis=0), b, dims)
    return both[:rows] + both[rows:]


def inverse_factor(gram):
    n = gram.shape[0]
    row = lax.broadcasted_iota(jnp.int32, (n, n), 0)
    col = lax.broadcasted_iota(jnp.int32, (n, n), 1)
    work = jnp.concatenate([gram, (row == col).astype(F32)], axis=1)
    ids = lax.broadcasted_iota(jnp.int32, (n, 1), 0)
    scale = jnp.zeros((n, 1), F32)
    for k in range(n):
        pivot = work[k : k + 1, :]
        column = work[:, k : k + 1]
        d = work[k : k + 1, k : k + 1]
        scale = jnp.where(ids == k, d, scale)
        factor = jnp.where(ids > k, column / d, 0.0)
        work = work - factor * pivot
    return work[:, n:] * lax.rsqrt(scale)


def exchange_kernel(
    cfg,
    q_hbm, cot_hbm, acts_hbm, err_hbm, weight_hbm,
    grad_out, basis_out, q_out,
    q_ref, cot_ref, acts_ref, err_ref, weight_ref,
    term, core_in, x_in, dp_in, left_all,
    right_part, right_in, right_all,
    partial, partial_in, partial_x,
    load_sem, core_sem, x_sem, dp_sem, gather_sem, gx_sem, gcore_sem, r_sem, rg_sem, pc_sem, px_sem,
):
    n_dp, n_t, groups, width, qwidth, blocks, early = cfg
    n_x = n_t // 2
    rank, ff = q_ref.shape
    tokens = cot_ref.shape[0]
    rows_dp = rank // (n_dp // groups)
    me_dp, me_t = lax.axis_index("dp"), lax.axis_index("tensor")
    core, me_x = lax.rem(me_t, 2), lax.div(me_t, 2)
    mate = 1 - core
    per = rank // 8

    def send(src, dst, sems, index, dp, t):
        return pltpu.make_async_remote_copy(
            src_ref=src,
            dst_ref=dst,
            send_sem=sems.at[(0,) + index],
            recv_sem=sems.at[(1,) + index],
            device_id=(dp, t),
            device_id_type=pl.DeviceIdType.MESH,
        )

    def at_x(k):
        return lax.rem(me_x + k, n_x) * 2 + core

    def at_dp(k):
        return lax.rem(me_dp + k, n_dp)

    loads = [
        pltpu.make_async_copy(src, dst, load_sem.at[i])
        for i, (src, dst) in enumerate(
            ((q_hbm, q_ref), (cot_hbm, cot_ref), (acts_hbm, acts_ref), (err_hbm, err_ref), (weight_hbm, weight_ref))
        )
    ]
    for load in loads:
        load.start()

    barrier = pltpu.get_barrier_semaphore()
    peers = [(me_dp, me_x * 2 + mate)]
    peers += [(me_dp, at_x(k)) for k in range(1, n_x)]
    peers += [(at_dp(k), me_t) for k in range(1, n_dp)]
    for peer in peers:
        pl.semaphore_signal(barrier, inc=1, device_id=peer, device_id_type=pl.DeviceIdType.MESH)

    loads[0].wait()
    loads[1].wait()
    q_both = jnp.concatenate(halves(q_ref[...]), axis=0)
    t = dot(q_both, cot_ref[...], NT)
    t_both = jnp.concatenate(halves(t[:rank] + t[rank:]), axis=0)
    loads[2].wait()
    loads[3].wait()

    def term_block(b, half):
        x, g = b // groups, b % groups
        column = pl.multiple_of(((x * 2 + half) * groups + g) * width, width)
        cut = pl.ds(column, width)
        both = dot(q_both, err_ref[cut, :], NT) + dot(t_both, acts_ref[:, cut], NN)
        value = both[:rank] + both[rank:]
        term[pl.ds((half * n_x * groups + b) * per, per)] = value.reshape(per, 8, width)

    for b in range(n_x * groups):
        term_block(b, mate)
    pl.semaphore_wait(barrier, len(peers))
    half_len = n_x * n_dp
    to_core = send(term.at[pl.ds(mate * half_len, half_len)], core_in, core_sem, (0,), me_dp, me_x * 2 + mate)
    to_core.start()
    for b in range(n_x * groups):
        term_block(b, core)
    to_core.wait()
    own_half = pl.ds(core * half_len, half_len)
    term[own_half] = term[own_half] + core_in[...]
    to_x = []
    for k in range(1, n_x):
        target = lax.rem(me_x + k, n_x)
        copy = send(
            term.at[pl.ds(core * half_len + target * n_dp, n_dp)], x_in.at[k], x_sem, (k,), me_dp, at_x(k)
        )
        copy.start()
        to_x.append(copy)

    loads[4].wait()
    dwidth = partial.shape[-1]

    def to_mate(b):
        return send(partial.at[b, pl.ds(mate * n_x, n_x)], partial_in.at[b], pc_sem, (b,), me_dp, me_x * 2 + mate)

    def product(b, _):
        cut = pl.ds(pl.multiple_of(b * dwidth, dwidth), dwidth)
        value = dot(cot_ref[...], weight_ref[cut, :], NT)
        step = tokens // n_t
        for tt in range(n_t):
            partial[b, (tt % 2) * n_x + tt // 2] = value[tt * step : (tt + 1) * step]
        to_mate(b).start()
        return 0

    lax.fori_loop(0, blocks, product, 0)

    own = pl.ds(core * half_len + me_x * n_dp, n_dp)
    for k, copy in enumerate(to_x, 1):
        copy.wait()
        term[own] = term[own] + x_in[k]
    to_dp = []
    for k in range(1, n_dp):
        copy = send(
            term.at[core * half_len + me_x * n_dp + at_dp(k)], dp_in.at[k], dp_sem, (k,), at_dp(k), me_t
        )
        copy.start()
        to_dp.append(copy)

    def x_copy(b, k):
        target = lax.rem(me_x + k, n_x)
        return send(partial.at[b, core * n_x + target], partial_x.at[k, b], px_sem, (k, b), me_dp, at_x(k))

    def pair_sum(b, _):
        to_mate(b).wait()
        mine = pl.ds(core * n_x, n_x)
        partial[b, mine] = partial[b, mine] + partial_in[b]
        return 0

    def x_start(b, _):
        for k in range(1, n_x):
            x_copy(b, k).start()
        return 0

    lax.fori_loop(0, early, pair_sum, 0)
    lax.fori_loop(0, early, x_start, 0)

    total = term[core * half_len + me_x * n_dp + me_dp]
    for k, copy in enumerate(to_dp, 1):
        copy.wait()
        total = total + dp_in[k]
    base = me_t * n_dp
    left_all[base + me_dp] = total
    to_all = []
    for k in range(1, n_dp):
        copy = send(left_all.at[base + me_dp], left_all.at[base + me_dp], gather_sem, (k,), at_dp(k), me_t)
        copy.start()
        to_all.append(copy)
    lax.fori_loop(early, blocks, pair_sum, 0)
    for copy in to_all:
        copy.wait()
    quarter = left_all.at[pl.ds(base, n_dp)]
    gathers = []
    for k in range(1, n_x):
        copy = send(quarter, quarter, gx_sem, (k,), me_dp, at_x(k))
        copy.start()
        gathers.append(copy)
    first = send(quarter, quarter, gcore_sem, (0,), me_dp, me_x * 2 + mate)
    first.start()
    seconds = []
    for k, copy in enumerate(gathers, 1):
        copy.wait()
        source = lax.rem(me_x - k + n_x, n_x) * 2 + core
        ref = left_all.at[pl.ds(source * n_dp, n_dp)]
        second = send(ref, ref, gcore_sem, (k,), me_dp, me_x * 2 + mate)
        second.start()
        seconds.append(second)
    lax.fori_loop(early, blocks, x_start, 0)
    first.wait()
    for copy in seconds:
        copy.wait()

    n_blocks = n_t * groups

    def left_block(b):
        return left_all[b * per : (b + 1) * per].reshape(rank, width)

    gram = jnp.zeros((rank, rank), F32)
    for b in range(n_blocks):
        block = left_block(b)
        gram += dot(block, block, NT, HI)
    inverse = inverse_factor(gram)
    u = jnp.zeros((2 * rank, tokens), F32)
    right = jnp.zeros((2 * rank, ff), F32)
    for b in range(n_blocks):
        cut = pl.ds(b * width, width)
        basis = dot(inverse, left_block(b), NN, HI)
        basis_out[:, cut] = basis
        both = jnp.concatenate(halves(basis), axis=0)
        u += dot(both, acts_ref[:, cut], NT)
        right += dot(both, err_ref[cut, :], NN)
    right += dot(jnp.concatenate(halves(u[:rank] + u[rank:]), axis=0), cot_ref[...], NN)
    right = right[:rank] + right[rank:]

    q_groups = n_dp // per
    right_part[...] = jnp.zeros_like(right_part)
    for g in range(q_groups):
        size = min(qwidth, ff - g * qwidth)
        piece = right[:, g * qwidth : g * qwidth + size]
        right_part[pl.ds(g * per, per), :, pl.ds(0, size)] = piece.reshape(per, 8, size)
    copies = []
    for k in range(1, n_dp):
        copy = send(right_part.at[at_dp(k)], right_in.at[k], r_sem, (k,), at_dp(k), me_t)
        copy.start()
        copies.append(copy)
    total = right_part[me_dp]
    for k, copy in enumerate(copies, 1):
        copy.wait()
        total = total + right_in[k]
    right_all[me_dp] = total * (1.0 / n_dp)
    copies = []
    for k in range(1, n_dp):
        copy = send(right_all.at[me_dp], right_all.at[me_dp], rg_sem, (k,), at_dp(k), me_t)
        copy.start()
        copies.append(copy)
    for copy in copies:
        copy.wait()
    for g in range(q_groups):
        size = min(qwidth, ff - g * qwidth)
        q_out[:, pl.ds(g * qwidth, size)] = right_all[pl.ds(g * per, per), :, pl.ds(0, size)].reshape(rank, size)

    def finish(b, _):
        value = partial[b, core * n_x + me_x]
        for k in range(1, n_x):
            x_copy(b, k).wait()
            value = value + partial_x[k, b]
        grad_out[:, pl.ds(pl.multiple_of(b * dwidth, dwidth), dwidth)] = value.astype(BF16)
        return 0

    lax.fori_loop(0, blocks, finish, 0)


def error_kernel(basis_ref, q_ref, acts_ref, cot_ref, err_ref, out_ref):
    bh, bl = halves(basis_ref[...])
    qh, ql = halves(q_ref[...])
    approx = dot(
        jnp.concatenate([bh, bl, bh], axis=0), jnp.concatenate([qh, qh, ql], axis=0), TN
    )
    merged = dot(acts_ref[...], cot_ref[...], TN) + err_ref[...].astype(F32)
    out_ref[...] = (merged - approx).astype(BF16)


def exchange(acts, cot, weight, err, q):
    n_dp, n_t = lax.axis_size("dp"), lax.axis_size("tensor")
    tokens, d = acts.shape
    rank, ff = q.shape
    n_x, per = n_t // 2, rank // 8
    groups = n_dp // per
    width = d // (n_t * groups)
    qwidth = ff if groups == 1 else -(-ff // (groups * 128)) * 128
    blocks, early = 8, 2
    dwidth = d // blocks
    vmem, dma = pltpu.VMEM, pltpu.SemaphoreType.DMA
    any_spec = pl.BlockSpec(memory_space=pl.ANY)
    return pl.pallas_call(
        functools.partial(exchange_kernel, (n_dp, n_t, groups, width, qwidth, blocks, early)),
        in_specs=[any_spec] * 5,
        out_specs=[pl.BlockSpec(memory_space=VMEM)] * 3,
        out_shape=(
            jax.ShapeDtypeStruct((tokens // n_t, d), BF16),
            jax.ShapeDtypeStruct((rank, d), F32),
            jax.ShapeDtypeStruct((rank, ff), F32),
        ),
        scratch_shapes=[
            vmem(q.shape, F32), vmem(cot.shape, BF16), vmem(acts.shape, BF16),
            vmem(err.shape, BF16), vmem(weight.shape, BF16),
            vmem((n_t * n_dp, 8, width), F32), vmem((n_x * n_dp, 8, width), F32),
            vmem((n_x, n_dp, 8, width), F32), vmem((n_dp, 8, width), F32),
            vmem((n_t * n_dp, 8, width), F32),
            vmem((n_dp, 8, qwidth), F32), vmem((n_dp, 8, qwidth), F32), vmem((n_dp, 8, qwidth), F32),
            vmem((blocks, n_t, tokens // n_t, dwidth), F32),
            vmem((blocks, n_x, tokens // n_t, dwidth), F32),
            vmem((n_x, blocks, tokens // n_t, dwidth), F32),
            dma((5,)), dma((2, 1)), dma((2, n_x)), dma((2, n_dp)), dma((2, n_dp)), dma((2, n_x)),
            dma((2, n_x)), dma((2, n_dp)), dma((2, n_dp)), dma((2, blocks)), dma((2, n_x, blocks)),
        ],
        compiler_params=pltpu.CompilerParams(
            collective_id=0, has_side_effects=True, vmem_limit_bytes=56 * 1024 * 1024
        ),
        name="exchange",
    )(q, cot, acts, err, weight)


def body(acts, up_cot, up_weight, error_buf, q_init):
    tokens, d = acts.shape
    rank, ff = q_init.shape
    err = error_buf[0]
    input_grad, basis, q_factor = exchange(acts, up_cot, up_weight, err, q_init)
    tile = 512
    whole = lambda shape: pl.BlockSpec(shape, lambda i: (0, 0))
    cols = lambda rows: pl.BlockSpec((rows, tile), lambda i: (0, i))
    rows = pl.BlockSpec((tile, ff), lambda i: (i, 0))
    new_error = pl.pallas_call(
        error_kernel,
        grid=(d // tile,),
        in_specs=[cols(rank), whole((rank, ff)), cols(tokens), whole((tokens, ff)), rows],
        out_specs=rows,
        out_shape=jax.ShapeDtypeStruct((d, ff), BF16),
        compiler_params=PARAMS,
        name="new_error",
    )(basis, q_factor, acts, up_cot, err)
    return (input_grad, new_error[None], basis, q_factor)


def solution(mesh):
    return jax.shard_map(
        body,
        mesh=mesh,
        in_specs=(
            P("dp", None),
            P("dp", "tensor"),
            P(None, "tensor"),
            P("dp", None, "tensor"),
            P(None, "tensor"),
        ),
        out_specs=(P(("dp", "tensor"), None), P("dp", None, "tensor"), P(), P(None, "tensor")),
        check_vma=False,
    )
```

time: 300 us -> 90.1 us (0.30)
  waiting for transfers between devices: 192 us -> 0 us
  Pallas kernels: 0 us -> 86.5 us
  matrix products: 69 us -> 0 us
  other arithmetic: 15.7 us -> 0 us
  between operations: 15.6 us -> 0.67 us
  local copies, waits for them, and re-layouts: 6.42 us -> 2.64 us
    psum x2 -> x0, waiting for transfers between devices: 192 us -> none  [the longest x1 132 us: body(): left = lax.psum(left_term, ('dp', 'tensor'))]
    pallas_call x0 -> x2, Pallas kernels: none -> 86.5 us  [the longest x1 72.9 us: exchange(): pl.pallas_call(functools.partial(exchange_kernel, (n_dp, n_t, groups, wid...]
    dot_general x6 -> x0, matrix products: 66.8 us -> none  [the longest x1 15.8 us: body(): lax.dot_general(basis, q_factor, (((0,), (0,)), ((), ())), precision=high...]
    another operation x5 -> x0, other arithmetic: 12.1 us -> none  [the longest x3 6.52 us: body(): chol = jnp.linalg.cholesky(gram)]
    unnamed x10 -> x9, local copies, waits for them, and re-layouts: 6.35 us -> 2.64 us
  transfers between devices with their start and end apart: 3 -> 0, of which waited for: 2 -> 0; matrix products, arithmetic and copies ran while one was open for 9% -> 0% of each run, Pallas kernels for 0% -> 0%
where the time goes in v1:
time: 90.1 us; the launch traced here: 89.8 us
  Pallas kernels  86.5 us (96%)
  local copies, waits for them, and re-layouts  2.64 us (3%)
    pallas_call x1, Pallas kernels, exchange(): pl.pallas_call(functools.partial(exchange_kernel, (n_dp, n_t, groups, wid...  72.9 us
    pallas_call x1, Pallas kernels, body(): pl.pallas_call(error_kernel, grid=(d // tile,), in_specs=[cols(rank), who...  13.6 us
    unnamed x9, local copies, waits for them, and re-layouts  2.64 us

profile of v1, /device:TPU:0, one launch (start us, length us, event | category | flops | bytes accessed | tf_op | source)
XLA Modules:
  0.0 89.8 jit_solution(1773277759241019269)
XLA Ops:
  0.6 72.9 %exchange.1 = (bf16[128,4096]{1,0:T(8,128)(2,1)}, f32[64,4096]{1,0:T(8,128)}, f32[64,896]{1,0:T(8,128)}) custom-call(f32[64,896]{1,0:T(8,128)} %q_hbm.1, bf16[512,896]{1,0:T(8,128)(2,1)} %cot_ref.1, bf16[512,4096]{1,0:T(8,128)(2,1)} %acts_ref.1, bf16[4096,896]{1,0:T(8,128)(2,1)} %bitcast.2, bf16[4096,896]{1,0:T(8,128)(2,1)} %weight_hbm.1), custom_call_target="tpu_custom_call" | custom-call | tf_op jit(solution)/shard_map/exchange/pallas_call | solution.py:305
  73.5 0.0 copy-start.1
  73.5 0.0 copy-start
  73.5 0.0 copy-start.2
  73.5 13.6 %new_error.1 = bf16[4096,896]{1,0:T(8,128)(2,1)} custom-call(f32[64,4096]{1,0:T(8,128)} %get-tuple-element.16.basis_ref, f32[64,896]{1,0:T(8,128)} %get-tuple-element.17.q_ref, bf16[512,4096]{1,0:T(8,128)(2,1)} %acts_ref.1, bf16[512,896]{1,0:T(8,128)(2,1)} %cot_ref.1, bf16[4096,896]{1,0:T(8,128)(2,1)} %bitcast.3), custom_call_target="tpu_custom_call" | custom-call | tf_op jit(solution)/shard_map/new_error/pallas_call | solution.py:343
  87.2 0.0 copy-done.1
  87.2 1.0 %copy.12 = bf16[128,4096]{1,0:T(8,128)(2,1)} copy(bf16[128,4096]{1,0:T(8,128)(2,1)S(1)} %copy-done.1) | data formatting | bytes 2097152
  88.1 0.0 copy-done
  88.1 1.0 %copy.13 = f32[64,4096]{1,0:T(8,128)} copy(f32[64,4096]{1,0:T(8,128)S(1)} %copy-done) | data formatting | bytes 2097152
  89.1 0.0 copy-done.2
  89.1 0.7 copy.14
Async XLA Ops:
  73.5 13.7 %copy-start.1 = (bf16[128,4096]{1,0:T(8,128)(2,1)S(1)}, bf16[128,4096]{1,0:T(8,128)(2,1)}, u32[]{:S(2)}) copy-start(bf16[128,4096]{1,0:T(8,128)(2,1)} %get-tuple-element.14) | copy-start | bytes 3145732
  73.5 14.6 %copy-start = (f32[64,4096]{1,0:T(8,128)S(1)}, f32[64,4096]{1,0:T(8,128)}, u32[]{:S(2)}) copy-start(f32[64,4096]{1,0:T(8,128)} %get-tuple-element.16.basis_ref) | copy-start | bytes 3145732
  73.5 15.6 %copy-start.2 = (f32[64,896]{1,0:T(8,128)S(1)}, f32[64,896]{1,0:T(8,128)}, u32[]{:S(2)}) copy-start(f32[64,896]{1,0:T(8,128)} %get-tuple-element.17.q_ref) | copy-start | bytes 688132

commit v2 on v1

--- a/solution.py
+++ b/solution.py
@@ -9,9 +9,7 @@
 
 F32 = jnp.float32
 BF16 = jnp.bfloat16
-HI = lax.Precision.HIGHEST
 VMEM = pltpu.VMEM
-PARAMS = pltpu.CompilerParams(vmem_limit_bytes=56 * 1024 * 1024)
 NT = (((1,), (1,)), ((), ()))
 NN = (((1,), (0,)), ((), ()))
 TN = (((0,), (0,)), ((), ()))
@@ -31,6 +29,13 @@
     rows = x.shape[0]
     both = dot(jnp.concatenate(halves(x), axis=0), b, dims)
     return both[:rows] + both[rows:]
+
+
+def thirds(x):
+    high, rest = x.astype(BF16), x
+    rest = x - high.astype(F32)
+    mid, low = halves(rest)
+    return high, mid, low
 
 
 def inverse_factor(gram):
@@ -53,11 +58,11 @@
 def exchange_kernel(
     cfg,
     q_hbm, cot_hbm, acts_hbm, err_hbm, weight_hbm,
-    grad_out, basis_out, q_out,
+    grad_out, basis_out, q_out, error_out,
     q_ref, cot_ref, acts_ref, err_ref, weight_ref,
     term, core_in, x_in, dp_in, left_all,
     right_part, right_in, right_all,
-    partial, partial_in, partial_x,
+    partial, partial_in, partial_x, merged, out_sem,
     load_sem, core_sem, x_sem, dp_sem, gather_sem, gx_sem, gcore_sem, r_sem, rg_sem, pc_sem, px_sem,
 ):
     n_dp, n_t, groups, width, qwidth, blocks, early = cfg
@@ -92,7 +97,7 @@
             ((q_hbm, q_ref), (cot_hbm, cot_ref), (acts_hbm, acts_ref), (err_hbm, err_ref), (weight_hbm, weight_ref))
         )
     ]
-    for load in loads:
+    for load in loads[:4]:
         load.start()
 
     barrier = pltpu.get_barrier_semaphore()
@@ -109,6 +114,7 @@
     t_both = jnp.concatenate(halves(t[:rank] + t[rank:]), axis=0)
     loads[2].wait()
     loads[3].wait()
+    loads[4].start()
 
     def term_block(b, half):
         x, g = b // groups, b % groups
@@ -144,16 +150,37 @@
     def to_mate(b):
         return send(partial.at[b, pl.ds(mate * n_x, n_x)], partial_in.at[b], pc_sem, (b,), me_dp, me_x * 2 + mate)
 
-    def product(b, _):
+    def product(b):
         cut = pl.ds(pl.multiple_of(b * dwidth, dwidth), dwidth)
         value = dot(cot_ref[...], weight_ref[cut, :], NT)
         step = tokens // n_t
         for tt in range(n_t):
             partial[b, (tt % 2) * n_x + tt // 2] = value[tt * step : (tt + 1) * step]
         to_mate(b).start()
-        return 0
-
-    lax.fori_loop(0, blocks, product, 0)
+
+    def x_copy(b, k):
+        target = lax.rem(me_x + k, n_x)
+        return send(
+            partial.at[b, core * n_x + target], partial_x.at[k - 1, b], px_sem, (k, b), me_dp, at_x(k)
+        )
+
+    def pair_sum(b):
+        to_mate(b).wait()
+        mine = pl.ds(core * n_x, n_x)
+        partial[b, mine] = partial[b, mine] + partial_in[b]
+
+    def x_start(b, _):
+        for k in range(1, n_x):
+            x_copy(b, k).start()
+        return 0
+
+    def step(b, _):
+        product(b)
+        pair_sum(b - 1)
+        return 0
+
+    product(0)
+    lax.fori_loop(1, blocks, step, 0)
 
     own = pl.ds(core * half_len + me_x * n_dp, n_dp)
     for k, copy in enumerate(to_x, 1):
@@ -167,74 +194,68 @@
         copy.start()
         to_dp.append(copy)
 
-    def x_copy(b, k):
-        target = lax.rem(me_x + k, n_x)
-        return send(partial.at[b, core * n_x + target], partial_x.at[k, b], px_sem, (k, b), me_dp, at_x(k))
-
-    def pair_sum(b, _):
-        to_mate(b).wait()
-        mine = pl.ds(core * n_x, n_x)
-        partial[b, mine] = partial[b, mine] + partial_in[b]
-        return 0
-
-    def x_start(b, _):
-        for k in range(1, n_x):
-            x_copy(b, k).start()
-        return 0
-
-    lax.fori_loop(0, early, pair_sum, 0)
     lax.fori_loop(0, early, x_start, 0)
-
+    pair_sum(blocks - 1)
+
+    mtile = 512
+
+    def merge(j, _):
+        cut = pl.ds(pl.multiple_of(j * mtile, mtile), mtile)
+        merged[cut, :] = dot(acts_ref[:, cut], cot_ref[...], TN) + err_ref[cut, :].astype(F32)
+        return 0
+
+    n_tiles = merged.shape[0] // mtile
     total = term[core * half_len + me_x * n_dp + me_dp]
     for k, copy in enumerate(to_dp, 1):
         copy.wait()
         total = total + dp_in[k]
-    base = me_t * n_dp
-    left_all[base + me_dp] = total
-    to_all = []
-    for k in range(1, n_dp):
-        copy = send(left_all.at[base + me_dp], left_all.at[base + me_dp], gather_sem, (k,), at_dp(k), me_t)
-        copy.start()
-        to_all.append(copy)
-    lax.fori_loop(early, blocks, pair_sum, 0)
-    for copy in to_all:
-        copy.wait()
-    quarter = left_all.at[pl.ds(base, n_dp)]
+    left_all[core, me_dp, me_x] = total
     gathers = []
     for k in range(1, n_x):
-        copy = send(quarter, quarter, gx_sem, (k,), me_dp, at_x(k))
+        piece = left_all.at[core, me_dp, me_x]
+        copy = send(piece, piece, gx_sem, (k,), me_dp, at_x(k))
         copy.start()
         gathers.append(copy)
-    first = send(quarter, quarter, gcore_sem, (0,), me_dp, me_x * 2 + mate)
-    first.start()
-    seconds = []
-    for k, copy in enumerate(gathers, 1):
-        copy.wait()
-        source = lax.rem(me_x - k + n_x, n_x) * 2 + core
-        ref = left_all.at[pl.ds(source * n_dp, n_dp)]
-        second = send(ref, ref, gcore_sem, (k,), me_dp, me_x * 2 + mate)
-        second.start()
-        seconds.append(second)
+    for copy in gathers:
+        copy.wait()
+    to_all = []
+    mine = left_all.at[core, me_dp]
+    for k in range(1, n_dp):
+        copy = send(mine, mine, gather_sem, (k,), at_dp(k), me_t)
+        copy.start()
+        to_all.append(copy)
+    forward = [send(mine, mine, gcore_sem, (0,), me_dp, me_x * 2 + mate)]
+    forward[0].start()
     lax.fori_loop(early, blocks, x_start, 0)
-    first.wait()
-    for copy in seconds:
+    lax.fori_loop(0, n_tiles // 2, merge, 0)
+    for k, copy in enumerate(to_all, 1):
+        copy.wait()
+        ref = left_all.at[core, lax.rem(me_dp - k + n_dp, n_dp)]
+        forward.append(send(ref, ref, gcore_sem, (k,), me_dp, me_x * 2 + mate))
+        forward[-1].start()
+    for copy in forward:
         copy.wait()
 
     n_blocks = n_t * groups
 
     def left_block(b):
-        return left_all[b * per : (b + 1) * per].reshape(rank, width)
-
-    gram = jnp.zeros((rank, rank), F32)
+        t, g = b // groups, b % groups
+        return left_all[t % 2, g * per : (g + 1) * per, t // 2].reshape(rank, width)
+
+    gram = jnp.zeros((3 * rank, 3 * rank), F32)
     for b in range(n_blocks):
-        block = left_block(b)
-        gram += dot(block, block, NT, HI)
-    inverse = inverse_factor(gram)
+        parts = jnp.concatenate(thirds(left_block(b)), axis=0)
+        gram += dot(parts, parts, NT)
+    gram = gram[:rank] + gram[rank : 2 * rank] + gram[2 * rank :]
+    gram = gram[:, :rank] + gram[:, rank : 2 * rank] + gram[:, 2 * rank :]
+    i0, i1, i2 = thirds(inverse_factor(gram))
+    inverse = jnp.concatenate([i0, i0, i1, i0, i1, i2], axis=1)
     u = jnp.zeros((2 * rank, tokens), F32)
     right = jnp.zeros((2 * rank, ff), F32)
     for b in range(n_blocks):
         cut = pl.ds(b * width, width)
-        basis = dot(inverse, left_block(b), NN, HI)
+        l0, l1, l2 = thirds(left_block(b))
+        basis = dot(inverse, jnp.concatenate([l0, l1, l0, l2, l1, l0], axis=0), NN)
         basis_out[:, cut] = basis
         both = jnp.concatenate(halves(basis), axis=0)
         u += dot(both, acts_ref[:, cut], NT)
@@ -253,6 +274,7 @@
         copy = send(right_part.at[at_dp(k)], right_in.at[k], r_sem, (k,), at_dp(k), me_t)
         copy.start()
         copies.append(copy)
+    lax.fori_loop(n_tiles // 2, 3 * n_tiles // 4, merge, 0)
     total = right_part[me_dp]
     for k, copy in enumerate(copies, 1):
         copy.wait()
@@ -263,31 +285,45 @@
         copy = send(right_all.at[me_dp], right_all.at[me_dp], rg_sem, (k,), at_dp(k), me_t)
         copy.start()
         copies.append(copy)
+    lax.fori_loop(3 * n_tiles // 4, n_tiles, merge, 0)
     for copy in copies:
         copy.wait()
     for g in range(q_groups):
         size = min(qwidth, ff - g * qwidth)
         q_out[:, pl.ds(g * qwidth, size)] = right_all[pl.ds(g * per, per), :, pl.ds(0, size)].reshape(rank, size)
+
+    qh, ql = halves(q_out[...])
+    q_parts = jnp.concatenate([qh, qh, ql], axis=0)
+
+    def store(j):
+        cut = pl.ds(pl.multiple_of(j * mtile, mtile), mtile)
+        return pltpu.make_async_copy(err_ref.at[cut, :], error_out.at[cut, :], out_sem.at[j])
+
+    def subtract(j, _):
+        cut = pl.ds(pl.multiple_of(j * mtile, mtile), mtile)
+        bh, bl = halves(basis_out[:, cut])
+        approx = dot(jnp.concatenate([bh, bl, bh], axis=0), q_parts, TN)
+        err_ref[cut, :] = (merged[cut, :] - approx).astype(BF16)
+        store(j).start()
+        return 0
+
+    lax.fori_loop(0, n_tiles, subtract, 0)
 
     def finish(b, _):
         value = partial[b, core * n_x + me_x]
         for k in range(1, n_x):
             x_copy(b, k).wait()
-            value = value + partial_x[k, b]
+            value = value + partial_x[k - 1, b]
         grad_out[:, pl.ds(pl.multiple_of(b * dwidth, dwidth), dwidth)] = value.astype(BF16)
         return 0
 
     lax.fori_loop(0, blocks, finish, 0)
 
-
-def error_kernel(basis_ref, q_ref, acts_ref, cot_ref, err_ref, out_ref):
-    bh, bl = halves(basis_ref[...])
-    qh, ql = halves(q_ref[...])
-    approx = dot(
-        jnp.concatenate([bh, bl, bh], axis=0), jnp.concatenate([qh, qh, ql], axis=0), TN
-    )
-    merged = dot(acts_ref[...], cot_ref[...], TN) + err_ref[...].astype(F32)
-    out_ref[...] = (merged - approx).astype(BF16)
+    def stored(j, _):
+        store(j).wait()
+        return 0
+
+    lax.fori_loop(0, n_tiles, stored, 0)
 
 
 def exchange(acts, cot, weight, err, q):
@@ -305,50 +341,36 @@
     return pl.pallas_call(
         functools.partial(exchange_kernel, (n_dp, n_t, groups, width, qwidth, blocks, early)),
         in_specs=[any_spec] * 5,
-        out_specs=[pl.BlockSpec(memory_space=VMEM)] * 3,
+        out_specs=[pl.BlockSpec(memory_space=VMEM)] * 3 + [any_spec],
         out_shape=(
             jax.ShapeDtypeStruct((tokens // n_t, d), BF16),
             jax.ShapeDtypeStruct((rank, d), F32),
             jax.ShapeDtypeStruct((rank, ff), F32),
+            jax.ShapeDtypeStruct((d, ff), BF16),
         ),
         scratch_shapes=[
             vmem(q.shape, F32), vmem(cot.shape, BF16), vmem(acts.shape, BF16),
             vmem(err.shape, BF16), vmem(weight.shape, BF16),
             vmem((n_t * n_dp, 8, width), F32), vmem((n_x * n_dp, 8, width), F32),
             vmem((n_x, n_dp, 8, width), F32), vmem((n_dp, 8, width), F32),
-            vmem((n_t * n_dp, 8, width), F32),
+            vmem((2, n_dp, n_x, 8, width), F32),
             vmem((n_dp, 8, qwidth), F32), vmem((n_dp, 8, qwidth), F32), vmem((n_dp, 8, qwidth), F32),
             vmem((blocks, n_t, tokens // n_t, dwidth), F32),
             vmem((blocks, n_x, tokens // n_t, dwidth), F32),
-            vmem((n_x, blocks, tokens // n_t, dwidth), F32),
+            vmem((n_x - 1, blocks, tokens // n_t, dwidth), F32),
+            vmem((d, ff), F32), dma((d // 512,)),
             dma((5,)), dma((2, 1)), dma((2, n_x)), dma((2, n_dp)), dma((2, n_dp)), dma((2, n_x)),
-            dma((2, n_x)), dma((2, n_dp)), dma((2, n_dp)), dma((2, blocks)), dma((2, n_x, blocks)),
+            dma((2, n_dp)), dma((2, n_dp)), dma((2, n_dp)), dma((2, blocks)), dma((2, n_x, blocks)),
         ],
         compiler_params=pltpu.CompilerParams(
-            collective_id=0, has_side_effects=True, vmem_limit_bytes=56 * 1024 * 1024
+            collective_id=0, has_side_effects=True, vmem_limit_bytes=61 * 1024 * 1024
         ),
         name="exchange",
     )(q, cot, acts, err, weight)
 
 
 def body(acts, up_cot, up_weight, error_buf, q_init):
-    tokens, d = acts.shape
-    rank, ff = q_init.shape
-    err = error_buf[0]
-    input_grad, basis, q_factor = exchange(acts, up_cot, up_weight, err, q_init)
-    tile = 512
-    whole = lambda shape: pl.BlockSpec(shape, lambda i: (0, 0))
-    cols = lambda rows: pl.BlockSpec((rows, tile), lambda i: (0, i))
-    rows = pl.BlockSpec((tile, ff), lambda i: (i, 0))
-    new_error = pl.pallas_call(
-        error_kernel,
-        grid=(d // tile,),
-        in_specs=[cols(rank), whole((rank, ff)), cols(tokens), whole((tokens, ff)), rows],
-        out_specs=rows,
-        out_shape=jax.ShapeDtypeStruct((d, ff), BF16),
-        compiler_params=PARAMS,
-        name="new_error",
-    )(basis, q_factor, acts, up_cot, err)
+    input_grad, basis, q_factor, new_error = exchange(acts, up_cot, up_weight, error_buf[0], q_init)
     return (input_grad, new_error[None], basis, q_factor)
 
 

time: 90.1 us -> 91.4 us (1.014)
  local copies, waits for them, and re-layouts: 2.64 us -> 10.8 us
  Pallas kernels: 86.5 us -> 79.8 us
    pallas_call x1 -> x0, Pallas kernels: 13.6 us -> none  [body(): pl.pallas_call(error_kernel, grid=(d // tile,), in_specs=[cols(rank), who...]
    unnamed x9 -> x8, local copies, waits for them, and re-layouts: 2.64 us -> 10.8 us
    pallas_call x1, Pallas kernels: 72.9 us -> 79.8 us  [exchange(): pl.pallas_call(functools.partial(exchange_kernel, (n_dp, n_t, groups, wid...]
where the time goes in v2:
time: 91.4 us; the launch traced here: 91.2 us
  Pallas kernels  79.8 us (87%)
  local copies, waits for them, and re-layouts  10.8 us (12%)
    pallas_call x1, Pallas kernels, exchange(): pl.pallas_call(functools.partial(exchange_kernel, (n_dp, n_t, groups, wid...  79.8 us
    unnamed x8, local copies, waits for them, and re-layouts  10.8 us

profile of v2, /device:TPU:0, one launch (start us, length us, event | category | flops | bytes accessed | tf_op | source)
XLA Modules:
  0.0 91.2 jit_solution(8923488353641582206)
XLA Ops:
  0.6 79.8 %exchange.1 = (bf16[128,4096]{1,0:T(8,128)(2,1)}, f32[64,4096]{1,0:T(8,128)}, f32[64,896]{1,0:T(8,128)}, bf16[4096,896]{1,0:T(8,128)(2,1)}) custom-call(f32[64,896]{1,0:T(8,128)} %q_hbm.1, bf16[512,896]{1,0:T(8,128)(2,1)} %cot_hbm.1, bf16[512,4096]{1,0:T(8,128)(2,1)} %acts_hbm.1, bf16[4096,896]{1,0:T(8,128)(2,1)} %bitcast.3, bf16[4096,896]{1,0:T(8,128)(2,1)} %weight_hbm.1), custom_call_target="tpu_custom_call" | custom-call | tf_op jit(solution)/shard_map/exchange/pallas_call | solution.py:341
  80.5 2.3 %copy.13 = bf16[128,4096]{1,0:T(8,128)(2,1)} copy(bf16[128,4096]{1,0:T(8,128)(2,1)} %get-tuple-element.16) | data formatting | bytes 2097152
  82.8 0.0 copy-start
  82.8 0.0 copy-start.1
  82.8 6.8 %copy.14 = bf16[1,4096,896]{2,1,0:T(8,128)(2,1)} copy(bf16[1,4096,896]{2,1,0:T(8,128)(2,1)} %bitcast.2) | data formatting | bytes 14680064
  89.6 0.0 copy-done
  89.6 1.0 %copy.15 = f32[64,4096]{1,0:T(8,128)} copy(f32[64,4096]{1,0:T(8,128)S(1)} %copy-done) | data formatting | bytes 2097152
  90.5 0.0 copy-done.1
  90.6 0.7 copy.16
Async XLA Ops:
  82.8 6.8 %copy-start = (f32[64,4096]{1,0:T(8,128)S(1)}, f32[64,4096]{1,0:T(8,128)}, u32[]{:S(2)}) copy-start(f32[64,4096]{1,0:T(8,128)} %get-tuple-element.18) | copy-start | bytes 3145732
  82.8 7.8 %copy-start.1 = (f32[64,896]{1,0:T(8,128)S(1)}, f32[64,896]{1,0:T(8,128)}, u32[]{:S(2)}) copy-start(f32[64,896]{1,0:T(8,128)} %get-tuple-element.19) | copy-start | bytes 688132

commit v3 on v2

--- a/solution.py
+++ b/solution.py
@@ -58,11 +58,11 @@
 def exchange_kernel(
     cfg,
     q_hbm, cot_hbm, acts_hbm, err_hbm, weight_hbm,
-    grad_out, basis_out, q_out, error_out,
+    grad_out, basis_out, q_out, flip_out,
     q_ref, cot_ref, acts_ref, err_ref, weight_ref,
     term, core_in, x_in, dp_in, left_all,
     right_part, right_in, right_all,
-    partial, partial_in, partial_x, merged, out_sem,
+    partial, partial_in, partial_x, flipped, out_sem,
     load_sem, core_sem, x_sem, dp_sem, gather_sem, gx_sem, gcore_sem, r_sem, rg_sem, pc_sem, px_sem,
 ):
     n_dp, n_t, groups, width, qwidth, blocks, early = cfg
@@ -199,12 +199,17 @@
 
     mtile = 512
 
-    def merge(j, _):
+    def store(j):
         cut = pl.ds(pl.multiple_of(j * mtile, mtile), mtile)
-        merged[cut, :] = dot(acts_ref[:, cut], cot_ref[...], TN) + err_ref[cut, :].astype(F32)
+        return pltpu.make_async_copy(flipped.at[cut, :], flip_out.at[cut, :], out_sem.at[j])
+
+    def flip(j, _):
+        cut = pl.ds(pl.multiple_of(j * mtile, mtile), mtile)
+        flipped[cut, :] = acts_ref[:, cut].T
+        store(j).start()
         return 0
 
-    n_tiles = merged.shape[0] // mtile
+    n_tiles = flipped.shape[0] // mtile
     total = term[core * half_len + me_x * n_dp + me_dp]
     for k, copy in enumerate(to_dp, 1):
         copy.wait()
@@ -227,7 +232,7 @@
     forward = [send(mine, mine, gcore_sem, (0,), me_dp, me_x * 2 + mate)]
     forward[0].start()
     lax.fori_loop(early, blocks, x_start, 0)
-    lax.fori_loop(0, n_tiles // 2, merge, 0)
+    lax.fori_loop(0, n_tiles, flip, 0)
     for k, copy in enumerate(to_all, 1):
         copy.wait()
         ref = left_all.at[core, lax.rem(me_dp - k + n_dp, n_dp)]
@@ -274,7 +279,6 @@
         copy = send(right_part.at[at_dp(k)], right_in.at[k], r_sem, (k,), at_dp(k), me_t)
         copy.start()
         copies.append(copy)
-    lax.fori_loop(n_tiles // 2, 3 * n_tiles // 4, merge, 0)
     total = right_part[me_dp]
     for k, copy in enumerate(copies, 1):
         copy.wait()
@@ -285,29 +289,11 @@
         copy = send(right_all.at[me_dp], right_all.at[me_dp], rg_sem, (k,), at_dp(k), me_t)
         copy.start()
         copies.append(copy)
-    lax.fori_loop(3 * n_tiles // 4, n_tiles, merge, 0)
     for copy in copies:
         copy.wait()
     for g in range(q_groups):
         size = min(qwidth, ff - g * qwidth)
         q_out[:, pl.ds(g * qwidth, size)] = right_all[pl.ds(g * per, per), :, pl.ds(0, size)].reshape(rank, size)
-
-    qh, ql = halves(q_out[...])
-    q_parts = jnp.concatenate([qh, qh, ql], axis=0)
-
-    def store(j):
-        cut = pl.ds(pl.multiple_of(j * mtile, mtile), mtile)
-        return pltpu.make_async_copy(err_ref.at[cut, :], error_out.at[cut, :], out_sem.at[j])
-
-    def subtract(j, _):
-        cut = pl.ds(pl.multiple_of(j * mtile, mtile), mtile)
-        bh, bl = halves(basis_out[:, cut])
-        approx = dot(jnp.concatenate([bh, bl, bh], axis=0), q_parts, TN)
-        err_ref[cut, :] = (merged[cut, :] - approx).astype(BF16)
-        store(j).start()
-        return 0
-
-    lax.fori_loop(0, n_tiles, subtract, 0)
 
     def finish(b, _):
         value = partial[b, core * n_x + me_x]
@@ -324,6 +310,25 @@
         return 0
 
     lax.fori_loop(0, n_tiles, stored, 0)
+
+
+def error_kernel(
+    grad_ref, basis_ref, q_ref, flip_ref, cot_ref, err_ref, grad_out, out_ref, basis_out, q_out, rhs_ref
+):
+    tokens = cot_ref.shape[0]
+
+    @pl.when(pl.program_id(0) == 0)
+    def _():
+        qh, ql = halves(-q_ref[...])
+        rhs_ref[:tokens] = cot_ref[...]
+        q_out[...] = q_ref[...]
+        rhs_ref[tokens:] = jnp.concatenate([qh, qh, ql, ql], axis=0)
+
+    grad_out[...] = grad_ref[...]
+    basis_out[...] = basis_ref[...]
+    bh, bl = halves(basis_ref[...].T)
+    lhs = jnp.concatenate([flip_ref[...], bh, bl, bh, bl], axis=1)
+    out_ref[...] = (dot(lhs, rhs_ref[...], NN) + err_ref[...].astype(F32)).astype(BF16)
 
 
 def exchange(acts, cot, weight, err, q):
@@ -346,7 +351,7 @@
             jax.ShapeDtypeStruct((tokens // n_t, d), BF16),
             jax.ShapeDtypeStruct((rank, d), F32),
             jax.ShapeDtypeStruct((rank, ff), F32),
-            jax.ShapeDtypeStruct((d, ff), BF16),
+            jax.ShapeDtypeStruct((d, tokens), BF16),
         ),
         scratch_shapes=[
             vmem(q.shape, F32), vmem(cot.shape, BF16), vmem(acts.shape, BF16),
@@ -358,19 +363,44 @@
             vmem((blocks, n_t, tokens // n_t, dwidth), F32),
             vmem((blocks, n_x, tokens // n_t, dwidth), F32),
             vmem((n_x - 1, blocks, tokens // n_t, dwidth), F32),
-            vmem((d, ff), F32), dma((d // 512,)),
+            vmem((d, tokens), BF16), dma((d // 512,)),
             dma((5,)), dma((2, 1)), dma((2, n_x)), dma((2, n_dp)), dma((2, n_dp)), dma((2, n_x)),
             dma((2, n_dp)), dma((2, n_dp)), dma((2, n_dp)), dma((2, blocks)), dma((2, n_x, blocks)),
         ],
         compiler_params=pltpu.CompilerParams(
-            collective_id=0, has_side_effects=True, vmem_limit_bytes=61 * 1024 * 1024
+            collective_id=0, has_side_effects=True, vmem_limit_bytes=56 * 1024 * 1024
         ),
         name="exchange",
     )(q, cot, acts, err, weight)
 
 
 def body(acts, up_cot, up_weight, error_buf, q_init):
-    input_grad, basis, q_factor, new_error = exchange(acts, up_cot, up_weight, error_buf[0], q_init)
+    tokens, d = acts.shape
+    rank, ff = q_init.shape
+    err = error_buf[0]
+    input_grad, basis, q_factor, flipped = exchange(acts, up_cot, up_weight, err, q_init)
+    tile = 512
+    whole = lambda shape: pl.BlockSpec(shape, lambda i: (0, 0))
+    rows = lambda width: pl.BlockSpec((tile, width), lambda i: (i, 0))
+    cols = lambda height: pl.BlockSpec((height, tile), lambda i: (0, i))
+    input_grad, new_error, basis, q_factor = pl.pallas_call(
+        error_kernel,
+        grid=(d // tile,),
+        in_specs=[
+            cols(input_grad.shape[0]), cols(rank), whole((rank, ff)),
+            rows(tokens), whole((tokens, ff)), rows(ff),
+        ],
+        out_specs=[cols(input_grad.shape[0]), rows(ff), cols(rank), whole((rank, ff))],
+        out_shape=(
+            jax.ShapeDtypeStruct(input_grad.shape, BF16),
+            jax.ShapeDtypeStruct((d, ff), BF16),
+            jax.ShapeDtypeStruct((rank, d), F32),
+            jax.ShapeDtypeStruct((rank, ff), F32),
+        ),
+        scratch_shapes=[pltpu.VMEM((tokens + 4 * rank, ff), BF16)],
+        compiler_params=pltpu.CompilerParams(vmem_limit_bytes=56 * 1024 * 1024),
+        name="new_error",
+    )(input_grad, basis, q_factor, flipped, up_cot, err)
     return (input_grad, new_error[None], basis, q_factor)
 
 

time: 91.4 us -> 90.3 us (0.988)
  local copies, waits for them, and re-layouts: 10.8 us -> 0 us
  Pallas kernels: 79.8 us -> 89.3 us
    pallas_call x0 -> x1, Pallas kernels: none -> 13.8 us  [body(): pl.pallas_call(error_kernel, grid=(d // tile,), in_specs=[cols(input_grad...]
    unnamed x8 -> x0, local copies, waits for them, and re-layouts: 10.8 us -> none
    pallas_call x1, Pallas kernels: 79.8 us -> 75.5 us  [exchange(): pl.pallas_call(functools.partial(exchange_kernel, (n_dp, n_t, groups, wid...]
where the time goes in v3:
time: 90.3 us; the launch traced here: 89.9 us
  Pallas kernels  89.3 us (99%)
    pallas_call x1, Pallas kernels, exchange(): pl.pallas_call(functools.partial(exchange_kernel, (n_dp, n_t, groups, wid...  75.5 us
    pallas_call x1, Pallas kernels, body(): pl.pallas_call(error_kernel, grid=(d // tile,), in_specs=[cols(input_grad...  13.8 us

profile of v3, /device:TPU:0, one launch (start us, length us, event | category | flops | bytes accessed | tf_op | source)
XLA Modules:
  0.0 89.9 jit_solution(11954759442659973376)
XLA Ops:
  0.6 75.5 %exchange.1 = (bf16[128,4096]{1,0:T(8,128)(2,1)}, f32[64,4096]{1,0:T(8,128)}, f32[64,896]{1,0:T(8,128)}, bf16[4096,512]{1,0:T(8,128)(2,1)}) custom-call(f32[64,896]{1,0:T(8,128)} %q_hbm.1, bf16[512,896]{1,0:T(8,128)(2,1)} %cot_ref.1, bf16[512,4096]{1,0:T(8,128)(2,1)} %acts_hbm.1, bf16[4096,896]{1,0:T(8,128)(2,1)} %bitcast.2, bf16[4096,896]{1,0:T(8,128)(2,1)} %weight_hbm.1), custom_call_target="tpu_custom_call" | custom-call | tf_op jit(solution)/shard_map/exchange/pallas_call | solution.py:346
  76.1 13.8 %new_error.1 = (bf16[128,4096]{1,0:T(8,128)(2,1)}, bf16[4096,896]{1,0:T(8,128)(2,1)}, f32[64,4096]{1,0:T(8,128)}, f32[64,896]{1,0:T(8,128)}) custom-call(bf16[128,4096]{1,0:T(8,128)(2,1)} %get-tuple-element.12.grad_ref, f32[64,4096]{1,0:T(8,128)} %get-tuple-element.13.basis_ref, f32[64,896]{1,0:T(8,128)} %get-tuple-element.14.q_ref, ...), custom_call_target="tpu_custom_call" | custom-call | tf_op jit(solution)/shard_map/new_error/pallas_call | solution.py:386

commit v4 on v3

--- a/solution.py
+++ b/solution.py
@@ -43,26 +43,31 @@
     row = lax.broadcasted_iota(jnp.int32, (n, n), 0)
     col = lax.broadcasted_iota(jnp.int32, (n, n), 1)
     work = jnp.concatenate([gram, (row == col).astype(F32)], axis=1)
-    ids = lax.broadcasted_iota(jnp.int32, (n, 1), 0)
-    scale = jnp.zeros((n, 1), F32)
+    work = [work[i : i + 8] for i in range(0, n, 8)]
+    ids = lax.broadcasted_iota(jnp.int32, (8, 1), 0)
+    scales = [jnp.zeros((8, 1), F32) for _ in work]
     for k in range(n):
-        pivot = work[k : k + 1, :]
-        column = work[:, k : k + 1]
-        d = work[k : k + 1, k : k + 1]
-        scale = jnp.where(ids == k, d, scale)
-        factor = jnp.where(ids > k, column / d, 0.0)
-        work = work - factor * pivot
-    return work[:, n:] * lax.rsqrt(scale)
+        at, r = k // 8, k % 8
+        pivot = work[at][r : r + 1, :]
+        d = pivot[:, k : k + 1]
+        scales[at] = jnp.where(ids == r, d, scales[at])
+        scaled = pivot / d
+        for g in range(at, n // 8):
+            column = work[g][:, k : k + 1]
+            if g == at:
+                column = jnp.where(ids > r, column, 0.0)
+            work[g] = work[g] - column * scaled
+    return jnp.concatenate([w[:, n:] * lax.rsqrt(v) for w, v in zip(work, scales)], axis=0)
 
 
 def exchange_kernel(
     cfg,
     q_hbm, cot_hbm, acts_hbm, err_hbm, weight_hbm,
-    grad_out, basis_out, q_out, flip_out,
+    grad_out, basis_out, q_out,
     q_ref, cot_ref, acts_ref, err_ref, weight_ref,
     term, core_in, x_in, dp_in, left_all,
     right_part, right_in, right_all,
-    partial, partial_in, partial_x, flipped, out_sem,
+    partial, partial_in, partial_x,
     load_sem, core_sem, x_sem, dp_sem, gather_sem, gx_sem, gcore_sem, r_sem, rg_sem, pc_sem, px_sem,
 ):
     n_dp, n_t, groups, width, qwidth, blocks, early = cfg
@@ -91,14 +96,30 @@
     def at_dp(k):
         return lax.rem(me_dp + k, n_dp)
 
+    n_own = n_x * groups
+
+    def column_of(b, half):
+        x, g = b // groups, b % groups
+        return pl.multiple_of(((x * 2 + half) * groups + g) * width, width)
+
+    def chunk(b, half, index):
+        cut = pl.ds(column_of(b, half), width)
+        return (
+            pltpu.make_async_copy(err_hbm.at[cut, :], err_ref.at[cut, :], load_sem.at[3 + 2 * index]),
+            pltpu.make_async_copy(acts_hbm.at[:, cut], acts_ref.at[:, cut], load_sem.at[4 + 2 * index]),
+        )
+
     loads = [
         pltpu.make_async_copy(src, dst, load_sem.at[i])
-        for i, (src, dst) in enumerate(
-            ((q_hbm, q_ref), (cot_hbm, cot_ref), (acts_hbm, acts_ref), (err_hbm, err_ref), (weight_hbm, weight_ref))
-        )
+        for i, (src, dst) in enumerate(((q_hbm, q_ref), (cot_hbm, cot_ref), (weight_hbm, weight_ref)))
     ]
-    for load in loads[:4]:
-        load.start()
+    mate_chunks = [chunk(b, mate, b) for b in range(n_own)]
+    own_chunks = [chunk(b, core, n_own + b) for b in range(n_own)]
+    loads[0].start()
+    loads[1].start()
+    for pair in mate_chunks + own_chunks:
+        for copy in pair:
+            copy.start()
 
     barrier = pltpu.get_barrier_semaphore()
     peers = [(me_dp, me_x * 2 + mate)]
@@ -112,25 +133,25 @@
     q_both = jnp.concatenate(halves(q_ref[...]), axis=0)
     t = dot(q_both, cot_ref[...], NT)
     t_both = jnp.concatenate(halves(t[:rank] + t[rank:]), axis=0)
-    loads[2].wait()
-    loads[3].wait()
-    loads[4].start()
 
     def term_block(b, half):
-        x, g = b // groups, b % groups
-        column = pl.multiple_of(((x * 2 + half) * groups + g) * width, width)
-        cut = pl.ds(column, width)
+        cut = pl.ds(column_of(b, half), width)
         both = dot(q_both, err_ref[cut, :], NT) + dot(t_both, acts_ref[:, cut], NN)
         value = both[:rank] + both[rank:]
         term[pl.ds((half * n_x * groups + b) * per, per)] = value.reshape(per, 8, width)
 
-    for b in range(n_x * groups):
+    for b in range(n_own):
+        for copy in mate_chunks[b]:
+            copy.wait()
         term_block(b, mate)
+    loads[2].start()
     pl.semaphore_wait(barrier, len(peers))
     half_len = n_x * n_dp
     to_core = send(term.at[pl.ds(mate * half_len, half_len)], core_in, core_sem, (0,), me_dp, me_x * 2 + mate)
     to_core.start()
-    for b in range(n_x * groups):
+    for b in range(n_own):
+        for copy in own_chunks[b]:
+            copy.wait()
         term_block(b, core)
     to_core.wait()
     own_half = pl.ds(core * half_len, half_len)
@@ -144,7 +165,7 @@
         copy.start()
         to_x.append(copy)
 
-    loads[4].wait()
+    loads[2].wait()
     dwidth = partial.shape[-1]
 
     def to_mate(b):
@@ -174,13 +195,18 @@
             x_copy(b, k).start()
         return 0
 
-    def step(b, _):
+    def make(b, _):
         product(b)
-        pair_sum(b - 1)
         return 0
 
-    product(0)
-    lax.fori_loop(1, blocks, step, 0)
+    def add(b, _):
+        pair_sum(b)
+        return 0
+
+    lax.fori_loop(0, blocks // 2, make, 0)
+    pair_sum(0)
+    x_start(0, 0)
+    lax.fori_loop(blocks // 2, blocks, make, 0)
 
     own = pl.ds(core * half_len + me_x * n_dp, n_dp)
     for k, copy in enumerate(to_x, 1):
@@ -194,22 +220,10 @@
         copy.start()
         to_dp.append(copy)
 
-    lax.fori_loop(0, early, x_start, 0)
-    pair_sum(blocks - 1)
-
-    mtile = 512
-
-    def store(j):
-        cut = pl.ds(pl.multiple_of(j * mtile, mtile), mtile)
-        return pltpu.make_async_copy(flipped.at[cut, :], flip_out.at[cut, :], out_sem.at[j])
-
-    def flip(j, _):
-        cut = pl.ds(pl.multiple_of(j * mtile, mtile), mtile)
-        flipped[cut, :] = acts_ref[:, cut].T
-        store(j).start()
-        return 0
-
-    n_tiles = flipped.shape[0] // mtile
+    lax.fori_loop(1, early, add, 0)
+    lax.fori_loop(1, early, x_start, 0)
+    lax.fori_loop(early, blocks, add, 0)
+
     total = term[core * half_len + me_x * n_dp + me_dp]
     for k, copy in enumerate(to_dp, 1):
         copy.wait()
@@ -232,7 +246,6 @@
     forward = [send(mine, mine, gcore_sem, (0,), me_dp, me_x * 2 + mate)]
     forward[0].start()
     lax.fori_loop(early, blocks, x_start, 0)
-    lax.fori_loop(0, n_tiles, flip, 0)
     for k, copy in enumerate(to_all, 1):
         copy.wait()
         ref = left_all.at[core, lax.rem(me_dp - k + n_dp, n_dp)]
@@ -305,15 +318,9 @@
 
     lax.fori_loop(0, blocks, finish, 0)
 
-    def stored(j, _):
-        store(j).wait()
-        return 0
-
-    lax.fori_loop(0, n_tiles, stored, 0)
-
 
 def error_kernel(
-    grad_ref, basis_ref, q_ref, flip_ref, cot_ref, err_ref, grad_out, out_ref, basis_out, q_out, rhs_ref
+    grad_ref, basis_ref, q_ref, acts_ref, cot_ref, err_ref, grad_out, out_ref, basis_out, q_out, rhs_ref
 ):
     tokens = cot_ref.shape[0]
 
@@ -326,9 +333,9 @@
 
     grad_out[...] = grad_ref[...]
     basis_out[...] = basis_ref[...]
-    bh, bl = halves(basis_ref[...].T)
-    lhs = jnp.concatenate([flip_ref[...], bh, bl, bh, bl], axis=1)
-    out_ref[...] = (dot(lhs, rhs_ref[...], NN) + err_ref[...].astype(F32)).astype(BF16)
+    bh, bl = halves(basis_ref[...])
+    lhs = jnp.concatenate([acts_ref[...], bh, bl, bh, bl], axis=0)
+    out_ref[...] = (dot(lhs, rhs_ref[...], TN) + err_ref[...].astype(F32)).astype(BF16)
 
 
 def exchange(acts, cot, weight, err, q):
@@ -342,16 +349,15 @@
     blocks, early = 8, 2
     dwidth = d // blocks
     vmem, dma = pltpu.VMEM, pltpu.SemaphoreType.DMA
-    any_spec = pl.BlockSpec(memory_space=pl.ANY)
+    any_spec = pl.BlockSpec(memory_space=pltpu.HBM)
     return pl.pallas_call(
         functools.partial(exchange_kernel, (n_dp, n_t, groups, width, qwidth, blocks, early)),
         in_specs=[any_spec] * 5,
-        out_specs=[pl.BlockSpec(memory_space=VMEM)] * 3 + [any_spec],
+        out_specs=[pl.BlockSpec(memory_space=VMEM)] * 3,
         out_shape=(
             jax.ShapeDtypeStruct((tokens // n_t, d), BF16),
             jax.ShapeDtypeStruct((rank, d), F32),
             jax.ShapeDtypeStruct((rank, ff), F32),
-            jax.ShapeDtypeStruct((d, tokens), BF16),
         ),
         scratch_shapes=[
             vmem(q.shape, F32), vmem(cot.shape, BF16), vmem(acts.shape, BF16),
@@ -363,12 +369,11 @@
             vmem((blocks, n_t, tokens // n_t, dwidth), F32),
             vmem((blocks, n_x, tokens // n_t, dwidth), F32),
             vmem((n_x - 1, blocks, tokens // n_t, dwidth), F32),
-            vmem((d, tokens), BF16), dma((d // 512,)),
-            dma((5,)), dma((2, 1)), dma((2, n_x)), dma((2, n_dp)), dma((2, n_dp)), dma((2, n_x)),
+            dma((3 + 2 * n_t * groups,)), dma((2, 1)), dma((2, n_x)), dma((2, n_dp)), dma((2, n_dp)), dma((2, n_x)),
             dma((2, n_dp)), dma((2, n_dp)), dma((2, n_dp)), dma((2, blocks)), dma((2, n_x, blocks)),
         ],
         compiler_params=pltpu.CompilerParams(
-            collective_id=0, has_side_effects=True, vmem_limit_bytes=56 * 1024 * 1024
+            collective_id=0, has_side_effects=True, vmem_limit_bytes=43 * 1024 * 1024
         ),
         name="exchange",
     )(q, cot, acts, err, weight)
@@ -378,7 +383,7 @@
     tokens, d = acts.shape
     rank, ff = q_init.shape
     err = error_buf[0]
-    input_grad, basis, q_factor, flipped = exchange(acts, up_cot, up_weight, err, q_init)
+    input_grad, basis, q_factor = exchange(acts, up_cot, up_weight, err, q_init)
     tile = 512
     whole = lambda shape: pl.BlockSpec(shape, lambda i: (0, 0))
     rows = lambda width: pl.BlockSpec((tile, width), lambda i: (i, 0))
@@ -388,7 +393,7 @@
         grid=(d // tile,),
         in_specs=[
             cols(input_grad.shape[0]), cols(rank), whole((rank, ff)),
-            rows(tokens), whole((tokens, ff)), rows(ff),
+            cols(tokens), whole((tokens, ff)), rows(ff),
         ],
         out_specs=[cols(input_grad.shape[0]), rows(ff), cols(rank), whole((rank, ff))],
         out_shape=(
@@ -398,9 +403,9 @@
             jax.ShapeDtypeStruct((rank, ff), F32),
         ),
         scratch_shapes=[pltpu.VMEM((tokens + 4 * rank, ff), BF16)],
-        compiler_params=pltpu.CompilerParams(vmem_limit_bytes=56 * 1024 * 1024),
+        compiler_params=pltpu.CompilerParams(vmem_limit_bytes=16 * 1024 * 1024),
         name="new_error",
-    )(input_grad, basis, q_factor, flipped, up_cot, err)
+    )(input_grad, basis, q_factor, acts, up_cot, err)
     return (input_grad, new_error[None], basis, q_factor)
 
 

time: 90.3 us -> 82.2 us (0.910)
  Pallas kernels: 89.3 us -> 77 us
  local copies, waits for them, and re-layouts: 0 us -> 4.3 us
    pallas_call x1, Pallas kernels: 75.5 us -> 67 us  [exchange(): pl.pallas_call(functools.partial(exchange_kernel, (n_dp, n_t, groups, wid...]
    unnamed x0 -> x8, local copies, waits for them, and re-layouts: none -> 4.3 us
    pallas_call x1, Pallas kernels: 13.8 us -> 9.98 us  [body(): pl.pallas_call(error_kernel, grid=(d // tile,), in_specs=[cols(input_grad...]
where the time goes in v4:
time: 82.2 us; the launch traced here: 82 us
  Pallas kernels  77 us (94%)
  local copies, waits for them, and re-layouts  4.3 us (5%)
    pallas_call x1, Pallas kernels, exchange(): pl.pallas_call(functools.partial(exchange_kernel, (n_dp, n_t, groups, wid...  67 us
    pallas_call x1, Pallas kernels, body(): pl.pallas_call(error_kernel, grid=(d // tile,), in_specs=[cols(input_grad...  9.98 us
    unnamed x8, local copies, waits for them, and re-layouts  4.3 us

profile of v4, /device:TPU:0, one launch (start us, length us, event | category | flops | bytes accessed | tf_op | source)
XLA Modules:
  0.0 82.0 jit_solution(16558370241579533681)
XLA Ops:
  0.6 0.0 copy-start.1
  0.6 2.2 %copy-done.1 = bf16[512,4096]{1,0:T(8,128)(2,1)S(1)} copy-done((bf16[512,4096]{1,0:T(8,128)(2,1)S(1)}, bf16[512,4096]{1,0:T(8,128)(2,1)}, u32[]{:S(2)}) %copy-start.1) | copy-done | bytes 4194328
  2.8 0.0 copy-start.2
  2.8 1.2 %copy-done.2 = bf16[512,896]{1,0:T(8,128)(2,1)S(1)} copy-done((bf16[512,896]{1,0:T(8,128)(2,1)S(1)}, bf16[512,896]{1,0:T(8,128)(2,1)}, u32[]{:S(2)}) %copy-start.2) | copy-done | bytes 917528
  4.0 0.0 copy-start.3
  4.0 0.9 %copy-done.3 = f32[64,896]{1,0:T(8,128)S(1)} copy-done((f32[64,896]{1,0:T(8,128)S(1)}, f32[64,896]{1,0:T(8,128)}, u32[]{:S(2)}) %copy-start.3) | copy-done | bytes 229400
  4.9 0.0 copy-start
  4.9 67.0 %exchange.1 = (bf16[128,4096]{1,0:T(8,128)(2,1)S(1)}, f32[64,4096]{1,0:T(8,128)S(1)}, f32[64,896]{1,0:T(8,128)S(1)}) custom-call(f32[64,896]{1,0:T(8,128)S(1)} %copy-done.3, bf16[512,896]{1,0:T(8,128)(2,1)S(1)} %copy-done.2, bf16[512,4096]{1,0:T(8,128)(2,1)S(1)} %copy-done.1, bf16[4096,896]{1,0:T(8,128)(2,1)} %bitcast.2, bf16[4096,896]{1,0:T(8,128)(2,1)} %weight_hbm.1), custom_call_target="tpu_custom_call" | custom-call | tf_op jit(solution)/shard_map/exchange/pallas_call | solution.py:353
  72.0 0.0 copy-done
  72.0 10.0 %new_error.1 = (bf16[128,4096]{1,0:T(8,128)(2,1)}, bf16[4096,896]{1,0:T(8,128)(2,1)}, f32[64,4096]{1,0:T(8,128)}, f32[64,896]{1,0:T(8,128)}) custom-call(bf16[128,4096]{1,0:T(8,128)(2,1)S(1)} %get-tuple-element.11.grad_ref, f32[64,4096]{1,0:T(8,128)S(1)} %get-tuple-element.12.basis_ref, f32[64,896]{1,0:T(8,128)S(1)} %get-tuple-element.13.q_ref, ...), custom_call_target="tpu_custom_call" | custom-call | tf_op jit(solution)/shard_map/new_error/pallas_call | solution.py:391
Async XLA Ops:
  0.6 2.2 %copy-start.1 = (bf16[512,4096]{1,0:T(8,128)(2,1)S(1)}, bf16[512,4096]{1,0:T(8,128)(2,1)}, u32[]{:S(2)}) copy-start(bf16[512,4096]{1,0:T(8,128)(2,1)} %acts_ref.1) | copy-start | bytes 12582916
  2.8 1.2 %copy-start.2 = (bf16[512,896]{1,0:T(8,128)(2,1)S(1)}, bf16[512,896]{1,0:T(8,128)(2,1)}, u32[]{:S(2)}) copy-start(bf16[512,896]{1,0:T(8,128)(2,1)} %cot_ref.1) | copy-start | bytes 2752516
  4.0 0.9 %copy-start.3 = (f32[64,896]{1,0:T(8,128)S(1)}, f32[64,896]{1,0:T(8,128)}, u32[]{:S(2)}) copy-start(f32[64,896]{1,0:T(8,128)} %q_hbm.1) | copy-start | bytes 688132
  4.9 67.1 %copy-start = (bf16[1,4096,896]{2,1,0:T(8,128)(2,1)S(1)}, bf16[1,4096,896]{2,1,0:T(8,128)(2,1)}, u32[]{:S(2)}) copy-start(bf16[1,4096,896]{2,1,0:T(8,128)(2,1)} %param.8) | copy-start | bytes 22020100

commit v5 on v4

--- a/solution.py
+++ b/solution.py
@@ -260,26 +260,33 @@
         t, g = b // groups, b % groups
         return left_all[t % 2, g * per : (g + 1) * per, t // 2].reshape(rank, width)
 
+    def stacked(x):
+        return jnp.concatenate(thirds(x), axis=0)
+
+    def folded(x):
+        return x[:rank] + x[rank : 2 * rank] + x[2 * rank :]
+
+    def by_inverse(x):
+        a0, a1, a2 = thirds(x)
+        return dot(inverse, jnp.concatenate([a0, a1, a0, a2, a1, a0], axis=0), NN)
+
     gram = jnp.zeros((3 * rank, 3 * rank), F32)
     for b in range(n_blocks):
-        parts = jnp.concatenate(thirds(left_block(b)), axis=0)
+        parts = stacked(left_block(b))
         gram += dot(parts, parts, NT)
-    gram = gram[:rank] + gram[rank : 2 * rank] + gram[2 * rank :]
+    gram = folded(gram)
     gram = gram[:, :rank] + gram[:, rank : 2 * rank] + gram[:, 2 * rank :]
+    u = jnp.zeros((3 * rank, tokens), F32)
+    right = jnp.zeros((3 * rank, ff), F32)
+    for b in range(n_blocks):
+        cut = pl.ds(b * width, width)
+        parts = stacked(left_block(b))
+        u += dot(parts, acts_ref[:, cut], NT)
+        right += dot(parts, err_ref[cut, :], NN)
+    right += dot(stacked(folded(u)), cot_ref[...], NN)
     i0, i1, i2 = thirds(inverse_factor(gram))
     inverse = jnp.concatenate([i0, i0, i1, i0, i1, i2], axis=1)
-    u = jnp.zeros((2 * rank, tokens), F32)
-    right = jnp.zeros((2 * rank, ff), F32)
-    for b in range(n_blocks):
-        cut = pl.ds(b * width, width)
-        l0, l1, l2 = thirds(left_block(b))
-        basis = dot(inverse, jnp.concatenate([l0, l1, l0, l2, l1, l0], axis=0), NN)
-        basis_out[:, cut] = basis
-        both = jnp.concatenate(halves(basis), axis=0)
-        u += dot(both, acts_ref[:, cut], NT)
-        right += dot(both, err_ref[cut, :], NN)
-    right += dot(jnp.concatenate(halves(u[:rank] + u[rank:]), axis=0), cot_ref[...], NN)
-    right = right[:rank] + right[rank:]
+    right = by_inverse(folded(right))
 
     q_groups = n_dp // per
     right_part[...] = jnp.zeros_like(right_part)
@@ -292,6 +299,8 @@
         copy = send(right_part.at[at_dp(k)], right_in.at[k], r_sem, (k,), at_dp(k), me_t)
         copy.start()
         copies.append(copy)
+    for b in range(n_blocks):
+        basis_out[:, pl.ds(b * width, width)] = by_inverse(left_block(b))
     total = right_part[me_dp]
     for k, copy in enumerate(copies, 1):
         copy.wait()
@@ -346,7 +355,7 @@
     groups = n_dp // per
     width = d // (n_t * groups)
     qwidth = ff if groups == 1 else -(-ff // (groups * 128)) * 128
-    blocks, early = 8, 2
+    blocks, early = 8, 3
     dwidth = d // blocks
     vmem, dma = pltpu.VMEM, pltpu.SemaphoreType.DMA
     any_spec = pl.BlockSpec(memory_space=pltpu.HBM)

time: 82.2 us -> 84.6 us (1.029)
  Pallas kernels: 77 us -> 79.5 us
    pallas_call x1, Pallas kernels: 67 us -> 69.5 us  [exchange(): pl.pallas_call(functools.partial(exchange_kernel, (n_dp, n_t, groups, wid...]
where the time goes in v5:
time: 84.6 us; the launch traced here: 84.4 us
  Pallas kernels  79.5 us (94%)
  local copies, waits for them, and re-layouts  4.3 us (5%)
    pallas_call x1, Pallas kernels, exchange(): pl.pallas_call(functools.partial(exchange_kernel, (n_dp, n_t, groups, wid...  69.5 us
    pallas_call x1, Pallas kernels, body(): pl.pallas_call(error_kernel, grid=(d // tile,), in_specs=[cols(input_grad...  9.98 us
    unnamed x8, local copies, waits for them, and re-layouts  4.3 us

profile of v5, /device:TPU:0, one launch (start us, length us, event | category | flops | bytes accessed | tf_op | source)
XLA Modules:
  0.0 84.4 jit_solution(6668415665460582490)
XLA Ops:
  0.6 0.0 copy-start.1
  0.6 2.2 %copy-done.1 = bf16[512,4096]{1,0:T(8,128)(2,1)S(1)} copy-done((bf16[512,4096]{1,0:T(8,128)(2,1)S(1)}, bf16[512,4096]{1,0:T(8,128)(2,1)}, u32[]{:S(2)}) %copy-start.1) | copy-done | bytes 4194328
  2.8 0.0 copy-start.2
  2.8 1.2 %copy-done.2 = bf16[512,896]{1,0:T(8,128)(2,1)S(1)} copy-done((bf16[512,896]{1,0:T(8,128)(2,1)S(1)}, bf16[512,896]{1,0:T(8,128)(2,1)}, u32[]{:S(2)}) %copy-start.2) | copy-done | bytes 917528
  4.0 0.0 copy-start.3
  4.0 0.9 %copy-done.3 = f32[64,896]{1,0:T(8,128)S(1)} copy-done((f32[64,896]{1,0:T(8,128)S(1)}, f32[64,896]{1,0:T(8,128)}, u32[]{:S(2)}) %copy-start.3) | copy-done | bytes 229400
  4.9 0.0 copy-start
  4.9 69.5 %exchange.1 = (bf16[128,4096]{1,0:T(8,128)(2,1)S(1)}, f32[64,4096]{1,0:T(8,128)S(1)}, f32[64,896]{1,0:T(8,128)S(1)}) custom-call(f32[64,896]{1,0:T(8,128)S(1)} %copy-done.3, bf16[512,896]{1,0:T(8,128)(2,1)S(1)} %copy-done.2, bf16[512,4096]{1,0:T(8,128)(2,1)S(1)} %copy-done.1, bf16[4096,896]{1,0:T(8,128)(2,1)} %bitcast.2, bf16[4096,896]{1,0:T(8,128)(2,1)} %weight_hbm.1), custom_call_target="tpu_custom_call" | custom-call | tf_op jit(solution)/shard_map/exchange/pallas_call | solution.py:362
  74.4 0.0 copy-done
  74.4 10.0 %new_error.1 = (bf16[128,4096]{1,0:T(8,128)(2,1)}, bf16[4096,896]{1,0:T(8,128)(2,1)}, f32[64,4096]{1,0:T(8,128)}, f32[64,896]{1,0:T(8,128)}) custom-call(bf16[128,4096]{1,0:T(8,128)(2,1)S(1)} %get-tuple-element.11.grad_ref, f32[64,4096]{1,0:T(8,128)S(1)} %get-tuple-element.12.basis_ref, f32[64,896]{1,0:T(8,128)S(1)} %get-tuple-element.13.q_ref, ...), custom_call_target="tpu_custom_call" | custom-call | tf_op jit(solution)/shard_map/new_error/pallas_call | solution.py:400
Async XLA Ops:
  0.6 2.2 %copy-start.1 = (bf16[512,4096]{1,0:T(8,128)(2,1)S(1)}, bf16[512,4096]{1,0:T(8,128)(2,1)}, u32[]{:S(2)}) copy-start(bf16[512,4096]{1,0:T(8,128)(2,1)} %acts_ref.1) | copy-start | bytes 12582916
  2.8 1.2 %copy-start.2 = (bf16[512,896]{1,0:T(8,128)(2,1)S(1)}, bf16[512,896]{1,0:T(8,128)(2,1)}, u32[]{:S(2)}) copy-start(bf16[512,896]{1,0:T(8,128)(2,1)} %cot_ref.1) | copy-start | bytes 2752516
  4.0 0.9 %copy-start.3 = (f32[64,896]{1,0:T(8,128)S(1)}, f32[64,896]{1,0:T(8,128)}, u32[]{:S(2)}) copy-start(f32[64,896]{1,0:T(8,128)} %q_hbm.1) | copy-start | bytes 688132
  4.9 69.5 %copy-start = (bf16[1,4096,896]{2,1,0:T(8,128)(2,1)S(1)}, bf16[1,4096,896]{2,1,0:T(8,128)(2,1)}, u32[]{:S(2)}) copy-start(bf16[1,4096,896]{2,1,0:T(8,128)(2,1)} %param.8) | copy-start | bytes 22020100

commit v6 on v5

--- a/solution.py
+++ b/solution.py
@@ -355,7 +355,7 @@
     groups = n_dp // per
     width = d // (n_t * groups)
     qwidth = ff if groups == 1 else -(-ff // (groups * 128)) * 128
-    blocks, early = 8, 3
+    blocks, early = 8, 1
     dwidth = d // blocks
     vmem, dma = pltpu.VMEM, pltpu.SemaphoreType.DMA
     any_spec = pl.BlockSpec(memory_space=pltpu.HBM)

time: 84.6 us -> 81.1 us (0.959)
  Pallas kernels: 79.5 us -> 75.9 us
    pallas_call x1, Pallas kernels: 69.5 us -> 65.9 us  [exchange(): pl.pallas_call(functools.partial(exchange_kernel, (n_dp, n_t, groups, wid...]
where the time goes in v6:
time: 81.1 us; the launch traced here: 80.9 us
  Pallas kernels  75.9 us (94%)
  local copies, waits for them, and re-layouts  4.3 us (5%)
    pallas_call x1, Pallas kernels, exchange(): pl.pallas_call(functools.partial(exchange_kernel, (n_dp, n_t, groups, wid...  65.9 us
    pallas_call x1, Pallas kernels, body(): pl.pallas_call(error_kernel, grid=(d // tile,), in_specs=[cols(input_grad...  9.98 us
    unnamed x8, local copies, waits for them, and re-layouts  4.3 us

profile of v6, /device:TPU:0, one launch (start us, length us, event | category | flops | bytes accessed | tf_op | source)
XLA Modules:
  0.0 80.9 jit_solution(8946144746486064947)
XLA Ops:
  0.6 0.0 copy-start.1
  0.6 2.2 %copy-done.1 = bf16[512,4096]{1,0:T(8,128)(2,1)S(1)} copy-done((bf16[512,4096]{1,0:T(8,128)(2,1)S(1)}, bf16[512,4096]{1,0:T(8,128)(2,1)}, u32[]{:S(2)}) %copy-start.1) | copy-done | bytes 4194328
  2.8 0.0 copy-start.2
  2.8 1.2 %copy-done.2 = bf16[512,896]{1,0:T(8,128)(2,1)S(1)} copy-done((bf16[512,896]{1,0:T(8,128)(2,1)S(1)}, bf16[512,896]{1,0:T(8,128)(2,1)}, u32[]{:S(2)}) %copy-start.2) | copy-done | bytes 917528
  4.0 0.0 copy-start.3
  4.0 0.9 %copy-done.3 = f32[64,896]{1,0:T(8,128)S(1)} copy-done((f32[64,896]{1,0:T(8,128)S(1)}, f32[64,896]{1,0:T(8,128)}, u32[]{:S(2)}) %copy-start.3) | copy-done | bytes 229400
  4.9 0.0 copy-start
  4.9 65.9 %exchange.1 = (bf16[128,4096]{1,0:T(8,128)(2,1)S(1)}, f32[64,4096]{1,0:T(8,128)S(1)}, f32[64,896]{1,0:T(8,128)S(1)}) custom-call(f32[64,896]{1,0:T(8,128)S(1)} %copy-done.3, bf16[512,896]{1,0:T(8,128)(2,1)S(1)} %copy-done.2, bf16[512,4096]{1,0:T(8,128)(2,1)S(1)} %copy-done.1, bf16[4096,896]{1,0:T(8,128)(2,1)} %bitcast.2, bf16[4096,896]{1,0:T(8,128)(2,1)} %weight_hbm.1), custom_call_target="tpu_custom_call" | custom-call | tf_op jit(solution)/shard_map/exchange/pallas_call | solution.py:362
  70.9 0.0 copy-done
  70.9 10.0 %new_error.1 = (bf16[128,4096]{1,0:T(8,128)(2,1)}, bf16[4096,896]{1,0:T(8,128)(2,1)}, f32[64,4096]{1,0:T(8,128)}, f32[64,896]{1,0:T(8,128)}) custom-call(bf16[128,4096]{1,0:T(8,128)(2,1)S(1)} %get-tuple-element.11.grad_ref, f32[64,4096]{1,0:T(8,128)S(1)} %get-tuple-element.12.basis_ref, f32[64,896]{1,0:T(8,128)S(1)} %get-tuple-element.13.q_ref, ...), custom_call_target="tpu_custom_call" | custom-call | tf_op jit(solution)/shard_map/new_error/pallas_call | solution.py:400
Async XLA Ops:
  0.6 2.2 %copy-start.1 = (bf16[512,4096]{1,0:T(8,128)(2,1)S(1)}, bf16[512,4096]{1,0:T(8,128)(2,1)}, u32[]{:S(2)}) copy-start(bf16[512,4096]{1,0:T(8,128)(2,1)} %acts_ref.1) | copy-start | bytes 12582916
  2.8 1.2 %copy-start.2 = (bf16[512,896]{1,0:T(8,128)(2,1)S(1)}, bf16[512,896]{1,0:T(8,128)(2,1)}, u32[]{:S(2)}) copy-start(bf16[512,896]{1,0:T(8,128)(2,1)} %cot_ref.1) | copy-start | bytes 2752516
  4.0 0.9 %copy-start.3 = (f32[64,896]{1,0:T(8,128)S(1)}, f32[64,896]{1,0:T(8,128)}, u32[]{:S(2)}) copy-start(f32[64,896]{1,0:T(8,128)} %q_hbm.1) | copy-start | bytes 688132
  4.9 65.9 %copy-start = (bf16[1,4096,896]{2,1,0:T(8,128)(2,1)S(1)}, bf16[1,4096,896]{2,1,0:T(8,128)(2,1)}, u32[]{:S(2)}) copy-start(bf16[1,4096,896]{2,1,0:T(8,128)(2,1)} %param.8) | copy-start | bytes 22020100
